TPU v7x, 256 devices: a whole 4x4x8 slice. The times are simulated.
256 devices in a mesh: dp: 16 (over x_lo, z), ctx: 16 (over y, x_hi, core).
Axes of the slice: x: 4 (x_hi: 2, x_lo: 2; x = x_hi * 2 + x_lo), y: 4, z: 8, core: 2. Of those that a mesh axis runs over, the one named last changes fastest.
Arguments:
- hidden: bfloat16 [16, 2048, 4096], P('dp', 'ctx'), may hold values from -6 to 6
- value_weight: bfloat16 [4096, 512], P(('dp', 'ctx')), may hold values from -0.09375 to 0.09375
- queries: bfloat16 [16, 2048, 4096], P('dp', 'ctx'), may hold values from -4.5 to 4.5
- key_rows: bfloat16 [16, 2048, 512], P('dp', 'ctx'), may hold values from -4.5 to 4.5
- attn_saved: bfloat16 [16, 2048, 4096], P('dp', 'ctx'), may hold values from -3 to 3
- grad_out: bfloat16 [16, 2048, 4096], P('dp', 'ctx'), may hold values from -6 to 6
- doc_lengths: int32 [16, 8], P('dp'), may hold values from 1 to 1024, 2048 in all within a row
- routing: int32 [16, 2048], P('dp'), may hold values from 0 to 2047, as said below
- visible_blocks: int32 [16, 32, 32], P('dp'), may hold values from 0 to 1, as said below
Outputs:
- grad_query: bfloat16 [16, 2048, 4096], P('dp', 'ctx')
- grad_key: bfloat16 [16, 2048, 512], P('dp', 'ctx')
- grad_value_weight: float32 [4096, 512], P(('dp', 'ctx'))
Inputs may be any that keep to these rules, and one draw needn't show every extreme that they name: For each pack, routing is a permutation: the token at position i, held by device i // 128 of ctx, goes to owner slot routing[i], held by device routing[i] // 128 of ctx, so every owner device receives 128 tokens. At most 16 tokens of one device go to one owner device, and this bound is reached in every draw. visible_blocks[b, b] = 1 for every block b. `doc_lengths`: each pack's lengths sum to 2048; the longest is 1024.
All inputs are finite; a program needn't handle non-finite values.
Results may differ from a plain program's by a relative error of at most 0.023.
Values may be sent and summed in bfloat16 or wider, within the bound.
A program may use at most 128 MiB of HBM per device.

v0:
```python
import math
import jax
import jax.numpy as jnp
from jax import lax
from jax.sharding import PartitionSpec as P

QH = 32
KVH = 4
HD = 128
VB = 64
far_below = -1e30


def document_index(positions, doc_lengths):
    doc_ends = jnp.cumsum(doc_lengths)
    return jnp.sum((positions[:, None] >= doc_ends[None, :]).astype(jnp.int32), axis=1)


def merge_pairs(first, second):
    top = jnp.maximum(first[0], second[0])
    return (top, first[1] * jnp.exp(first[0] - top) + second[1] * jnp.exp(second[0] - top))


def local(
    hidden,
    value_weight,
    queries,
    key_rows,
    attn_saved,
    grad_out,
    doc_lengths,
    routing,
    visible_blocks,
):
    row_count = hidden.shape[1]
    ctx_count = lax.axis_size("ctx")
    dp_count = lax.axis_size("dp")
    ctx_place = lax.axis_index("ctx")
    token_count = routing.shape[1]
    capacity = 2 * row_count // ctx_count
    slot_count = ctx_count * capacity
    group_size = QH // KVH
    kv_width = key_rows.shape[2]
    score_scale = 1.0 / math.sqrt(HD)
    features = hidden[0]
    slot_route = routing[0]
    lengths = doc_lengths[0]
    block_table = visible_blocks[0].astype(jnp.float32)
    block_count = block_table.shape[0]
    columns = features
    projected = jnp.dot(
        columns,
        lax.all_gather(value_weight, ("dp", "ctx"), axis=0, tiled=True),
        preferred_element_type=jnp.float32,
    )
    value_rows = projected.astype(jnp.bfloat16)
    token_iota = jnp.arange(token_count, dtype=jnp.int32)
    slot_position = jnp.zeros((token_count,), jnp.int32).at[slot_route].set(token_iota)
    query_position = lax.dynamic_slice_in_dim(slot_position, ctx_place * row_count, row_count)
    local_route = lax.dynamic_slice_in_dim(slot_route, ctx_place * row_count, row_count)
    device_iota = jnp.arange(ctx_count, dtype=jnp.int32)
    target = local_route // row_count
    matches = (target[:, None] == device_iota[None, :]).astype(jnp.int32)
    earlier = jnp.cumsum(matches, axis=0) - matches
    send_slot = target * capacity + jnp.sum(earlier * matches, axis=1)
    buffer_iota = jnp.arange(slot_count, dtype=jnp.int32)
    send_matrix = (buffer_iota[:, None] == send_slot[None, :]).astype(jnp.bfloat16)
    owner_table = slot_route.reshape(ctx_count, row_count) // row_count
    coming = (owner_table == ctx_place).astype(jnp.int32)
    arrival = (device_iota[:, None] * capacity + jnp.cumsum(coming, axis=1) - coming).reshape(
        token_count
    )
    arrive_slot = arrival[query_position]
    receive_matrix = (arrive_slot[:, None] == buffer_iota[None, :]).astype(jnp.bfloat16)

    def to_slots(source_rows):
        placed = jnp.dot(send_matrix, source_rows, preferred_element_type=jnp.float32).astype(
            jnp.bfloat16
        )
        return placed.reshape(ctx_count, capacity, source_rows.shape[1])

    def from_slots(arrived):
        flat_rows = arrived.reshape(slot_count, arrived.shape[2])
        return jnp.dot(receive_matrix, flat_rows, preferred_element_type=jnp.float32).astype(
            jnp.bfloat16
        )

    local_pair = jnp.concatenate([key_rows[0], value_rows], axis=1)
    got_query, got_grad, got_pair = (
        lax.all_to_all(to_slots(queries[0]), "ctx", split_axis=0, concat_axis=0, tiled=True),
        lax.all_to_all(to_slots(grad_out[0]), "ctx", split_axis=0, concat_axis=0, tiled=True),
        lax.all_to_all(to_slots(local_pair), "ctx", split_axis=0, concat_axis=0, tiled=True),
    )
    pair_rows = from_slots(got_pair)
    owner_query = from_slots(got_query)
    owner_grad = from_slots(got_grad)
    pair_whole = lax.all_gather(pair_rows, "ctx", axis=0, tiled=True)
    query_docs = document_index(query_position, lengths)
    key_docs = document_index(slot_position, lengths)
    block_iota = jnp.arange(block_count, dtype=jnp.int32)
    query_onehot = (query_position[:, None] // VB == block_iota[None, :]).astype(jnp.float32)
    row_visible = jnp.dot(query_onehot, block_table, preferred_element_type=jnp.float32)
    key_onehot = (slot_position[:, None] // VB == block_iota[None, :]).astype(jnp.float32)
    visible = jnp.dot(row_visible, key_onehot.T, preferred_element_type=jnp.float32)
    allowed = (
        (query_docs[:, None] == key_docs[None, :])
        & (slot_position[None, :] <= query_position[:, None])
        & (visible > 0.5)
    )
    presence = jnp.broadcast_to(
        allowed.astype(jnp.float32)[None], (group_size, row_count, token_count)
    )
    query_heads = owner_query.reshape(row_count, KVH, group_size, HD)
    grad_heads = owner_grad.reshape(row_count, KVH, group_size, HD)
    saved_heads = attn_saved[0].astype(jnp.float32).reshape(row_count, KVH, group_size, HD)
    row_delta = jnp.transpose(
        jnp.sum(grad_heads.astype(jnp.float32) * saved_heads, axis=-1), (1, 2, 0)
    )
    key_all = pair_whole[:, :kv_width].reshape(token_count, KVH, HD)
    value_all = pair_whole[:, kv_width:].reshape(token_count, KVH, HD)
    query_parts = []
    key_parts = []
    value_parts = []
    for kv_head in range(KVH):
        head_query = query_heads[:, kv_head]
        head_grad = grad_heads[:, kv_head]
        head_keys = key_all[:, kv_head]
        scores = (
            jnp.einsum("rjd,kd->jrk", head_query, head_keys, preferred_element_type=jnp.float32)
            * score_scale
        )
        masked = jnp.where(allowed[None], scores, far_below)
        row_top, row_total = lax.reduce(
            (masked, presence), (jnp.float32(far_below), jnp.float32(0.0)), merge_pairs, (2,)
        )
        log_total = (row_top + jnp.log(row_total))[..., None]
        weights = jnp.where(allowed[None], jnp.exp(scores - log_total), 0.0)
        weights_b = weights.astype(jnp.bfloat16)
        dweights = jnp.einsum(
            "rjd,kd->jrk", head_grad, value_all[:, kv_head], preferred_element_type=jnp.float32
        ).astype(jnp.bfloat16)
        dscores = (
            score_scale * weights * (dweights.astype(jnp.float32) - row_delta[kv_head][..., None])
        ).astype(jnp.bfloat16)
        query_parts.append(
            jnp.einsum("jrk,kd->rjd", dscores, head_keys, preferred_element_type=jnp.float32)
        )
        key_parts.append(
            jnp.einsum("jrk,rjd->kd", dscores, head_query, preferred_element_type=jnp.float32)
        )
        value_parts.append(
            jnp.einsum("jrk,rjd->kd", weights_b, head_grad, preferred_element_type=jnp.float32)
        )
    query_grad = jnp.stack(query_parts, axis=1)
    pair_terms = jnp.concatenate(
        [jnp.concatenate(key_parts, axis=1), jnp.concatenate(value_parts, axis=1)], axis=1
    )
    pair_sums = lax.psum_scatter(
        pair_terms.astype(jnp.bfloat16), "ctx", scatter_dimension=0, tiled=True
    )
    outgoing = jnp.dot(receive_matrix.T, pair_sums, preferred_element_type=jnp.float32).astype(
        jnp.bfloat16
    )
    returned = lax.all_to_all(
        outgoing.reshape(ctx_count, capacity, 2 * kv_width),
        "ctx",
        split_axis=0,
        concat_axis=0,
        tiled=True,
    )
    loader_grad = jnp.dot(
        send_matrix.T,
        returned.reshape(slot_count, 2 * kv_width),
        preferred_element_type=jnp.float32,
    ).astype(jnp.bfloat16)
    grad_value = loader_grad[:, kv_width:]
    weight_scale = 1.0 / math.sqrt(dp_count * token_count)
    columns = features
    weight_grad = lax.psum_scatter(
        jnp.einsum("rd,rk->dk", columns, grad_value, preferred_element_type=jnp.float32)
        * weight_scale,
        ("dp", "ctx"),
        scatter_dimension=0,
        tiled=True,
    )
    grad_query = query_grad.reshape(row_count, QH * HD).astype(jnp.bfloat16)
    return (grad_query[None], loader_grad[:, :kv_width][None], weight_grad)


def solution(mesh):
    placed = (
        P("dp", "ctx", None),
        P(("dp", "ctx"), None),
        P("dp", "ctx", None),
        P("dp", "ctx", None),
        P("dp", "ctx", None),
        P("dp", "ctx", None),
        P("dp", None),
        P("dp", None),
        P("dp", None, None),
    )
    return jax.shard_map(
        local,
        mesh=mesh,
        in_specs=placed,
        out_specs=(P("dp", "ctx", None), P("dp", "ctx", None), P(("dp", "ctx"), None)),
        check_vma=False,
    )
```

profile of v0, /device:TPU:128, one launch (start us, length us, event | category | flops | bytes accessed | tf_op | source)
XLA Modules:
  0.0 2082.8 jit_solution(7185739076317425619)
XLA Ops:
  8.6 8.0 scatter_custom_fusion
  19.3 405.7 %all-gather.3.cloned.1.call-done = bf16[4096,512]{1,0:T(8,128)(2,1)} async-done(((bf16[16,512]{1,0:T(8,128)(2,1)}), bf16[4096,512]{1,0:T(8,128)(2,1)}) %all-gather.3.cloned.1.call-update) | async-done | bytes 4194320 | tf_op jit(solution)/shard_map/all_gather | solution.py:53
  429.9 3.6 all-to-all-start
  435.8 10.0 all-to-all-done
  448.8 3.7 all-to-all-start.2
  452.6 3.3 convolution_convert_fusion.1
  455.8 28.8 %all-to-all-done.2 = bf16[16,16,4096]{2,1,0:T(8,128)(2,1)S(1)} async-done(((bf16[16,16,4096]{2,1,0:T(8,128)(2,1)}), bf16[16,16,4096]{2,1,0:T(8,128)(2,1)S(1)}, u32[]{:S(2)}, u32[]{:S(2)}) %all-to-all-start.2) | async-done | bytes 2097184 | tf_op jit(solution)/shard_map/all_to_all | solution.py:91
  484.6 4.4 all-to-all-start.1
  498.5 31.1 %all-to-all-done.1 = bf16[16,16,4096]{2,1,0:T(8,128)(2,1)} async-done(((bf16[16,16,4096]{2,1,0:T(8,128)(2,1)}), bf16[16,16,4096]{2,1,0:T(8,128)(2,1)}, u32[]{:S(2)}, u32[]{:S(2)}) %all-to-all-start.1) | async-done | bytes 2097184 | tf_op jit(solution)/shard_map/all_to_all | solution.py:90
  541.9 4.6 fusion.140
  546.5 4.1 reshape.213
  550.6 4.0 reshape.207
  554.6 8.9 fusion.142
  563.5 4.3 fusion.141
  569.1 3.4 fusion.17
  572.5 3.4 fusion.16
  579.6 3.4 fusion.7
  585.4 4.5 fusion.12
  592.5 4.7 fusion.2
  597.2 6.7 fusion.11
  606.3 6.2 fusion.6
  612.5 4.5 fusion.53
  617.0 4.3 fusion.1
  625.6 3.8 fusion.68
  637.4 6.4 copy.240
  643.9 85.8 %reduce-scatter.7.cloned.1.call-done = bf16[128,1024]{1,0:T(8,128)(2,1)} async-done(((bf16[2048,1024]{1,0:T(8,128)(2,1)}), bf16[128,1024]{1,0:T(8,128)(2,1)}) %reduce-scatter.7.cloned.1.call-update) | async-done | bytes 262160
  731.0 16.4 all_to_all.20
  747.7 4.5 multiply_bitcast_fusion
  752.2 9.0 copy.242
  761.3 3.4 fusion.83
  764.7 3.7 fusion.85
  772.1 1303.9 %reduce-scatter.9.cloned.1.call-done = f32[16,512]{1,0:T(8,128)} async-done(((f32[4096,512]{1,0:T(8,128)}), f32[16,512]{1,0:T(8,128)}) %reduce-scatter.9.cloned.1.call-update) | async-done | bytes 32784
  (132 shorter events, 65.7 us)
Async XLA Ops:
  7.2 417.8 %copy-start = (bf16[1,128,4096]{2,1,0:T(8,128)(2,1)S(1)}, bf16[1,128,4096]{2,1,0:T(8,128)(2,1)}, u32[]{:S(2)}) copy-start(bf16[1,128,4096]{2,1,0:T(8,128)(2,1)} %param.9) | copy-start | bytes 3145732
  7.2 439.6 %copy-start.21 = (bf16[1,128,4096]{2,1,0:T(8,128)(2,1)S(1)}, bf16[1,128,4096]{2,1,0:T(8,128)(2,1)}, u32[]{:S(2)}) copy-start(bf16[1,128,4096]{2,1,0:T(8,128)(2,1)} %param.14) | copy-start | bytes 3145732
  7.2 417.8 %all-gather.3.cloned.1.call-start = ((), (), s32[]{:S(2)}) async-start(), calls=%async_computation.6 | async-start | bytes 4210688 | tf_op jit(solution)/shard_map/all_gather | solution.py:53
  429.9 15.9 all-to-all-start
  433.4 55.7 %copy-start.28 = (s32[1,8]{1,0:T(1,128)S(1)}, s32[1,8]{1,0:T(1,128)}, u32[]{:S(2)}) copy-start(s32[1,8]{1,0:T(1,128)} %param.15) | copy-start | bytes 100
  433.5 56.1 %copy-start.27 = (s32[1,32,32]{2,1,0:T(8,128)S(1)}, s32[1,32,32]{2,1,0:T(8,128)}, u32[]{:S(2)}) copy-start(s32[1,32,32]{2,1,0:T(8,128)} %param.17) | copy-start | bytes 12292
  433.5 108.5 %all-gather.5.cloned.1.call-start = ((), (), s32[]{:S(2)}) async-start(), calls=%async_computation.7 | async-start | bytes 4456448 | tf_op jit(solution)/shard_map/all_gather | solution.py:97
  448.8 35.8 %all-to-all-start.2 = ((bf16[16,16,4096]{2,1,0:T(8,128)(2,1)}), bf16[16,16,4096]{2,1,0:T(8,128)(2,1)S(1)}, u32[]{:S(2)}, u32[]{:S(2)}) async-start(bf16[16,16,4096]{2,1,0:T(8,128)(2,1)} %bitcast.340), calls=%async_computation.2 | async-start | bytes 4194304 | tf_op jit(solution)/shard_map/all_to_all | solution.py:91
  484.6 6.9 copy-start.8
  484.6 44.9 %all-to-all-start.1 = ((bf16[16,16,4096]{2,1,0:T(8,128)(2,1)}), bf16[16,16,4096]{2,1,0:T(8,128)(2,1)}, u32[]{:S(2)}, u32[]{:S(2)}) async-start(bf16[16,16,4096]{2,1,0:T(8,128)(2,1)} %bitcast.338), calls=%async_computation.1 | async-start | bytes 4194304 | tf_op jit(solution)/shard_map/all_to_all | solution.py:90
  489.1 240.6 %reduce-scatter.7.cloned.1.call-start = ((), (), s32[]{:S(2)}) async-start(), calls=%async_computation.8 | async-start | bytes 4456448
  494.5 85.1 %copy-start.10 = (pred[128,2048]{0,1:T(8,128)(4,1)}, pred[128,2048]{0,1:T(8,128)(4,1)S(1)}, u32[]{:S(2)}) copy-start(pred[128,2048]{0,1:T(8,128)(4,1)S(1)} %copy.165) | copy-start | bytes 786436
  541.9 36.3 %copy-start.18 = (bf16[128,1,8,128]{3,2,1,0:T(8,128)(2,1)}, bf16[128,1,8,128]{3,2,1,0:T(8,128)(2,1)S(1)}, u32[]{:S(2)}) copy-start(bf16[128,1,8,128]{3,2,1,0:T(8,128)(2,1)S(1)} %get-tuple-element.51) | copy-start | bytes 786436
  554.6 8.9 copy-start.2
  563.5 5.6 copy-start.16
  563.5 14.8 copy-start.14
  567.9 4.6 copy-start.26
  585.4 4.5 copy-start.1
  597.2 6.7 copy-start.20
  597.2 9.1 copy-start.11
  603.9 8.6 copy-start.4
  606.3 6.2 copy-start.19
  606.3 10.7 copy-start.22
  617.0 6.3 copy-start.17
  623.3 6.1 slice-start
  623.3 6.1 copy-start.25
  625.6 3.8 slice-start.1
  643.8 1432.2 %reduce-scatter.9.cloned.1.call-start = ((), (), s32[]{:S(2)}) async-start(), calls=%async_computation.9 | async-start | bytes 8421376
  761.2 7.2 copy-start.13
  761.2 7.2 copy-start.5
  761.3 7.9 copy-start.7
  761.3 7.9 copy-start.12
  (6 other events, 16.4 us)
Sparse Core Ops, SparseCore 0:
  9.9 414.9 all-gather.2
  446.9 80.7 all-gather.4
  644.0 85.6 reduce-scatter.6
  761.4 1314.6 reduce-scatter.8
where the time goes:
time: 2090 us; the launch traced here: 2080 us
  waiting for transfers between devices  1870 us (89%)
  matrix products  81.8 us (4%)
  local copies, waits for them, and re-layouts  67.4 us (3%)
  other arithmetic  24.6 us (1%)
    unnamed x6, waiting for transfers between devices  1390 us
    all_gather x1, waiting for transfers between devices, local(): lax.all_gather(value_weight, ('dp', 'ctx'), axis=0, tiled=True)  406 us
  transfers between devices with their start and end apart: 7, of which 6 were waited for; matrix products, arithmetic and copies ran while one was open for 2% of the time, Pallas kernels for 0%

commit v1 on v0

--- a/solution.py
+++ b/solution.py
@@ -50,7 +50,12 @@
     columns = features
     projected = jnp.dot(
         columns,
-        lax.all_gather(value_weight, ("dp", "ctx"), axis=0, tiled=True),
+        jnp.concatenate(
+            lax.all_to_all(
+                jnp.stack([value_weight] * lax.axis_size(("dp", "ctx"))), ("dp", "ctx"), 0, 0
+            ),
+            axis=0,
+        ),
         preferred_element_type=jnp.float32,
     )
     value_rows = projected.astype(jnp.bfloat16)

time: 2090 us -> 1790 us (0.86)
  waiting for transfers between devices: 1870 us -> 1540 us
    all_gather x1 -> x0, waiting for transfers between devices: 406 us -> none  [local(): lax.all_gather(value_weight, ('dp', 'ctx'), axis=0, tiled=True)]
    all_to_all x0 -> x1, waiting for transfers between devices: none -> 83.2 us  [local(): lax.all_to_all(jnp.stack([value_weight] * lax.axis_size(('dp', 'ctx'))),...]
    unnamed x6 -> x5, waiting for transfers between devices: 1390 us -> 1390 us
  transfers between devices with their start and end apart: 7 -> 7, of which waited for: 6 -> 6; matrix products, arithmetic and copies ran while one was open for 2% -> 3% of each run, Pallas kernels for 0% -> 0%
where the time goes in v1:
time: 1790 us; the launch traced here: 1780 us
  waiting for transfers between devices  1540 us (86%)
  matrix products  81.2 us (5%)
  local copies, waits for them, and re-layouts  70.8 us (4%)
  starting transfers between devices  27.5 us (2%)
  other arithmetic  21 us (1%)
    unnamed x5, waiting for transfers between devices  1390 us
    all_to_all x1, waiting for transfers between devices, local(): lax.all_to_all(jnp.stack([value_weight] * lax.axis_size(('dp', 'ctx'))),...  83.2 us
  transfers between devices with their start and end apart: 7, of which 6 were waited for; matrix products, arithmetic and copies ran while one was open for 3% of the time, Pallas kernels for 0%

profile of v1, /device:TPU:128, one launch (start us, length us, event | category | flops | bytes accessed | tf_op | source)
XLA Modules:
  0.0 1776.2 jit_solution(10640993222210446982)
XLA Ops:
  10.5 14.8 all-to-all-start
  25.4 8.0 scatter_custom_fusion
  34.0 83.2 %all-to-all-done = bf16[256,16,512]{2,1,0:T(8,128)(2,1)} async-done(((bf16[256,16,512]{2,1,0:T(8,128)(2,1)}), bf16[256,16,512]{2,1,0:T(8,128)(2,1)}, u32[]{:S(2)}, u32[]{:S(2)}) %all-to-all-start) | async-done | bytes 4194336 | tf_op jit(solution)/shard_map/all_to_all | solution.py:54
  121.2 4.4 all-to-all-start.1
  127.3 10.8 all-to-all-done.1
  141.1 3.7 all-to-all-start.3
  148.0 28.8 %all-to-all-done.3 = bf16[16,16,4096]{2,1,0:T(8,128)(2,1)S(1)} async-done(((bf16[16,16,4096]{2,1,0:T(8,128)(2,1)}), bf16[16,16,4096]{2,1,0:T(8,128)(2,1)S(1)}, u32[]{:S(2)}, u32[]{:S(2)}) %all-to-all-start.3) | async-done | bytes 2097184 | tf_op jit(solution)/shard_map/all_to_all | solution.py:96
  176.9 4.4 all-to-all-start.2
  190.8 31.0 %all-to-all-done.2 = bf16[16,16,4096]{2,1,0:T(8,128)(2,1)} async-done(((bf16[16,16,4096]{2,1,0:T(8,128)(2,1)}), bf16[16,16,4096]{2,1,0:T(8,128)(2,1)}, u32[]{:S(2)}, u32[]{:S(2)}) %all-to-all-start.2) | async-done | bytes 2097184 | tf_op jit(solution)/shard_map/all_to_all | solution.py:95
  234.2 4.6 fusion.140
  238.7 4.2 reshape.219
  242.9 4.0 reshape.213
  246.9 8.9 fusion.142
  255.8 4.3 fusion.141
  261.4 3.4 fusion.17
  264.8 3.6 fusion.16
  272.0 3.4 fusion.7
  277.9 4.5 fusion.12
  284.9 4.5 fusion.2
  289.4 6.7 fusion.11
  298.5 6.2 fusion.6
  304.8 4.5 fusion.53
  309.3 4.4 fusion.1
  317.9 3.8 fusion.68
  329.7 6.4 copy.240
  336.2 86.7 %reduce-scatter.7.cloned.1.call-done = bf16[128,1024]{1,0:T(8,128)(2,1)} async-done(((bf16[2048,1024]{1,0:T(8,128)(2,1)}), bf16[128,1024]{1,0:T(8,128)(2,1)}) %reduce-scatter.7.cloned.1.call-update) | async-done | bytes 262160
  424.2 16.5 all_to_all.25
  441.0 4.5 multiply_bitcast_fusion
  445.4 9.0 copy.242
  454.5 3.4 fusion.83
  457.9 3.7 fusion.85
  465.3 1303.9 %reduce-scatter.9.cloned.1.call-done = f32[16,512]{1,0:T(8,128)} async-done(((f32[4096,512]{1,0:T(8,128)}), f32[16,512]{1,0:T(8,128)}) %reduce-scatter.9.cloned.1.call-update) | async-done | bytes 32784
  (136 shorter events, 67.4 us)
Async XLA Ops:
  7.2 110.0 %copy-start = (bf16[1,128,4096]{2,1,0:T(8,128)(2,1)S(1)}, bf16[1,128,4096]{2,1,0:T(8,128)(2,1)}, u32[]{:S(2)}) copy-start(bf16[1,128,4096]{2,1,0:T(8,128)(2,1)} %param.9) | copy-start | bytes 3145732
  7.2 18.2 %copy-start.28 = (s32[1,2048]{1,0:T(1,128)S(1)}, s32[1,2048]{1,0:T(1,128)}, u32[]{:S(2)}) copy-start(s32[1,2048]{1,0:T(1,128)} %param.16) | copy-start | bytes 24580
  7.2 112.9 %copy-start.27 = (bf16[1,128,512]{2,1,0:T(8,128)(2,1)S(1)}, bf16[1,128,512]{2,1,0:T(8,128)(2,1)}, u32[]{:S(2)}) copy-start(bf16[1,128,512]{2,1,0:T(8,128)(2,1)} %param.12) | copy-start | bytes 393220
  10.5 128.5 %copy-start.21 = (bf16[1,128,4096]{2,1,0:T(8,128)(2,1)S(1)}, bf16[1,128,4096]{2,1,0:T(8,128)(2,1)}, u32[]{:S(2)}) copy-start(bf16[1,128,4096]{2,1,0:T(8,128)(2,1)} %param.14) | copy-start | bytes 3145732
  10.5 106.7 %all-to-all-start = ((bf16[256,16,512]{2,1,0:T(8,128)(2,1)}), bf16[256,16,512]{2,1,0:T(8,128)(2,1)}, u32[]{:S(2)}, u32[]{:S(2)}) async-start(bf16[256,16,512]{2,1,0:T(8,128)(2,1)} %stack.17), calls=%async_computation | async-start | bytes 8388608 | tf_op jit(solution)/shard_map/all_to_all | solution.py:54
  121.2 16.8 all-to-all-start.1
  125.6 55.7 %copy-start.30 = (s32[1,8]{1,0:T(1,128)S(1)}, s32[1,8]{1,0:T(1,128)}, u32[]{:S(2)}) copy-start(s32[1,8]{1,0:T(1,128)} %param.15) | copy-start | bytes 100
  125.7 56.1 %copy-start.29 = (s32[1,32,32]{2,1,0:T(8,128)S(1)}, s32[1,32,32]{2,1,0:T(8,128)}, u32[]{:S(2)}) copy-start(s32[1,32,32]{2,1,0:T(8,128)} %param.17) | copy-start | bytes 12292
  125.7 108.5 %all-gather.2.cloned.1.call-start = ((), (), s32[]{:S(2)}) async-start(), calls=%async_computation.7 | async-start | bytes 4456448 | tf_op jit(solution)/shard_map/all_gather | solution.py:102
  141.1 35.8 %all-to-all-start.3 = ((bf16[16,16,4096]{2,1,0:T(8,128)(2,1)}), bf16[16,16,4096]{2,1,0:T(8,128)(2,1)S(1)}, u32[]{:S(2)}, u32[]{:S(2)}) async-start(bf16[16,16,4096]{2,1,0:T(8,128)(2,1)} %bitcast.341), calls=%async_computation.3 | async-start | bytes 4194304 | tf_op jit(solution)/shard_map/all_to_all | solution.py:96
  176.9 6.9 copy-start.8
  176.9 44.9 %all-to-all-start.2 = ((bf16[16,16,4096]{2,1,0:T(8,128)(2,1)}), bf16[16,16,4096]{2,1,0:T(8,128)(2,1)}, u32[]{:S(2)}, u32[]{:S(2)}) async-start(bf16[16,16,4096]{2,1,0:T(8,128)(2,1)} %bitcast.339), calls=%async_computation.2 | async-start | bytes 4194304 | tf_op jit(solution)/shard_map/all_to_all | solution.py:95
  181.3 241.6 %reduce-scatter.7.cloned.1.call-start = ((), (), s32[]{:S(2)}) async-start(), calls=%async_computation.8 | async-start | bytes 4456448
  186.8 85.2 %copy-start.10 = (pred[128,2048]{0,1:T(8,128)(4,1)}, pred[128,2048]{0,1:T(8,128)(4,1)S(1)}, u32[]{:S(2)}) copy-start(pred[128,2048]{0,1:T(8,128)(4,1)S(1)} %copy.165) | copy-start | bytes 786436
  234.2 36.6 %copy-start.18 = (bf16[128,1,8,128]{3,2,1,0:T(8,128)(2,1)}, bf16[128,1,8,128]{3,2,1,0:T(8,128)(2,1)S(1)}, u32[]{:S(2)}) copy-start(bf16[128,1,8,128]{3,2,1,0:T(8,128)(2,1)S(1)} %get-tuple-element.51) | copy-start | bytes 786436
  246.9 8.9 copy-start.2
  255.8 5.6 copy-start.16
  255.8 15.0 copy-start.14
  260.1 4.6 copy-start.26
  289.4 6.7 copy-start.20
  289.4 9.1 copy-start.11
  296.2 8.6 copy-start.4
  298.5 6.2 copy-start.19
  298.5 10.7 copy-start.22
  309.3 6.3 copy-start.17
  315.6 6.1 slice-start
  315.6 6.1 copy-start.25
  336.1 1433.1 %reduce-scatter.9.cloned.1.call-start = ((), (), s32[]{:S(2)}) async-start(), calls=%async_computation.9 | async-start | bytes 8421376
  454.4 7.2 copy-start.13
  454.5 7.2 copy-start.5
  454.5 8.0 copy-start.7
  454.5 8.0 copy-start.12
  (8 other events, 24.7 us)
Sparse Core Ops, SparseCore 0:
  139.1 81.7 all-gather.1
  336.3 86.5 reduce-scatter.6
  454.6 1314.5 reduce-scatter.8
